TPU v7x, 32 devices: a whole 2x2x4 slice. The times are simulated.
32 devices in a mesh: shots: 2 (over y), lat: 4 (over z), depth: 4 (over x, core).
Axes of the slice: x: 2, y: 2, z: 4, core: 2. Of those that a mesh axis runs over, the one named last changes fastest.
Arguments:
- source: float32 [8, 32, 1024], P('shots', 'lat'), parts along dimension 0, may hold values from -6 to 6
- traces: float32 [64, 4096], P(('shots', 'lat')), parts along dimension 0, may hold values from -6 to 6
- trace_tiles: int32 [64, 1], P(('shots', 'lat')), parts along dimension 0, may hold values from 0 to 3; in each aligned block of 8 rows (0 to 7, 8 to 15, ...) at most 5 rows name the same one
- trace_offsets: int32 [64], P(('shots', 'lat')), parts along dimension 0, may hold values from 0 to 7
- stencil: float32 [4, 2, 9, 9], replicated, may hold values from -0.9 to 0.9
- angular_freq: float32 [4], replicated, may hold values from 2 to 6
- slowness: float32 [4, 16384], P('depth', 'lat'), may hold values from 0.5 to 2
- reflect: float32 [4, 16384], P('depth', 'lat'), may hold values from -4 to 4
Outputs:
- picture: float32 [8, 16384], P(('shots', 'depth'), 'lat'), parts along dimension 0
- residual: float32 [64, 4, 1024], P(('shots', 'lat', 'depth')), parts along dimension 0
There are 2 independent parts, one for each index of `shots`. A program takes and returns all parts, laid end to end along the dimension named above; an argument that names none is the same for every part. Nothing has to cross between parts.
Inputs may be any that keep to these rules, and one draw needn't show every extreme that they name: `trace_tiles`: among the 8 blocks of one device, at most 5 name the same tile; on some device one tile is named by exactly 5 of them.
All inputs are finite; a program needn't handle non-finite values.
Results may differ from a plain program's by a relative error of at most 0.00029.
Values sent between devices are 32-bit elements; how exact they have to be, the bound alone decides.
A program may use at most 64 MiB of HBM per device.

v0:
```python
import jax
import jax.numpy as jnp
from jax import lax
from jax.sharding import PartitionSpec as P

precision_high = lax.Precision.HIGHEST


def padded_2(array, sides, width):
    for axis, dim in sides:
        count, length = (lax.axis_size(axis), array.shape[dim])
        up = [(i, (i + 1) % count) for i in range(count - 1)]
        down = [(j, i) for i, j in up]
        last = lax.slice_in_dim(array, length - width, length, axis=dim)
        leading = lax.slice_in_dim(array, 0, width, axis=dim)
        before = lax.ppermute(last, axis, up)
        after = lax.ppermute(leading, axis, down)
        array = jnp.concatenate([before, array, after], axis=dim)
    return array


def from_behind(value, axis, steps):
    count = lax.axis_size(axis)
    leading, last = (max(0, -steps), min(count, count - steps))
    return lax.ppermute(value, axis, [(source, source + steps) for source in range(leading, last)])


def broadcast(block, axis, holder):
    block = jnp.where(lax.axis_index(axis) == holder, block, jnp.zeros_like(block))
    return lax.psum(block, axis)


def make_taps(stencil):
    adjoint = jnp.stack([stencil[:, 0, ::-1, ::-1], -stencil[:, 1, ::-1, ::-1]], axis=1)
    return (stencil, adjoint)


def rotate(wave_field, phase_angle, direction):
    half_width = phase_angle.shape[-1]
    cosine = jnp.cos(phase_angle)
    sine_part = direction * jnp.sin(phase_angle)
    real_part = wave_field[..., :half_width]
    imag_part = wave_field[..., half_width:]
    return jnp.concatenate(
        [real_part * cosine - imag_part * sine_part, real_part * sine_part + imag_part * cosine],
        axis=-1,
    )


def convolve(wave_field, taps):
    tap_count = taps.shape[-1]
    tap_reach = tap_count // 2
    line_count = wave_field.shape[2]
    half_width = wave_field.shape[3] // 2
    padded = padded_2(wave_field, (("lat", 2),), tap_reach)
    widths = ((0, 0), (0, 0), (0, 0), (tap_reach, tap_reach))
    real_pad = jnp.pad(padded[..., :half_width], widths)
    imag_pad = jnp.pad(padded[..., half_width:], widths)
    out_shape = (wave_field.shape[0], wave_field.shape[1], line_count, half_width)
    out_real = jnp.zeros(out_shape, jnp.float32)
    out_imag = jnp.zeros(out_shape, jnp.float32)
    for row_tap in range(tap_count):
        for col_tap in range(tap_count):
            real_piece = real_pad[
                :, :, row_tap : row_tap + line_count, col_tap : col_tap + half_width
            ]
            imag_piece = imag_pad[
                :, :, row_tap : row_tap + line_count, col_tap : col_tap + half_width
            ]
            tap_real = taps[:, 0, row_tap, col_tap][None, :, None, None]
            tap_imag = taps[:, 1, row_tap, col_tap][None, :, None, None]
            out_real = out_real + tap_real * real_piece - tap_imag * imag_piece
            out_imag = out_imag + tap_imag * real_piece + tap_real * imag_piece
    return jnp.concatenate([out_real, out_imag], axis=-1)


def march_down(wave_field, op_table, angles):
    wave_field = rotate(convolve(wave_field, op_table), angles[0], 1.0)
    stored = [wave_field]
    return jnp.stack(stored)


def march_up(up_wave, op_table, angles, src_levels, model_pair):
    for step_index in reversed(range(angles.shape[0])):
        up_wave = up_wave + model_pair[step_index][None, None] * src_levels[step_index][None]
        up_wave = convolve(rotate(up_wave, angles[step_index], -1.0), op_table)
    return up_wave


def local(source, traces, trace_tiles, trace_offsets, stencil, angular_freq, slowness, reflect):
    freq_count, tile_rows, full_width = source.shape
    half_width = full_width // 2
    step_count = slowness.shape[0]
    depth_count = lax.axis_size("depth")
    depth_index = lax.axis_index("depth")
    forward, adjoint = make_taps(stencil)
    places = jnp.arange(tile_rows).astype(jnp.float32)
    targets = (trace_tiles[:, 0] * tile_rows + trace_offsets).astype(jnp.float32)
    lat_start = (lax.axis_index("lat") * tile_rows).astype(jnp.float32)
    piece_traces = lax.all_gather(traces, "lat", axis=0, tiled=True)
    piece_rows = lax.all_gather(targets, "lat", axis=0, tiled=True)
    selector = ((piece_rows - lat_start)[None, :] == places[:, None]).astype(jnp.float32)
    observed = jnp.dot(selector, piece_traces, precision=precision_high)
    observed = observed.reshape(tile_rows, freq_count, full_width)
    surface = jnp.transpose(observed, (1, 0, 2))
    receiver = jnp.concatenate([surface[..., :half_width], -surface[..., half_width:]], axis=-1)
    pair_fields = jnp.stack([source, receiver])
    level_slow = slowness.reshape(step_count, tile_rows, half_width)
    angles = angular_freq[None, :, None, None] * level_slow[:, None]
    model_half = reflect.reshape(step_count, tile_rows, half_width)
    model_pair = jnp.concatenate([model_half, model_half], axis=-1)
    top_slab = depth_index == 0
    top_input = jnp.where(top_slab, pair_fields, 0.0)

    def round_down(turn_index, current):
        bottom = march_down(current, forward, angles)[-1]
        return from_behind(bottom, "depth", 1) + top_input

    current = lax.fori_loop(0, depth_count - 1, round_down, top_input)
    levels = march_down(current, forward, angles)
    sources = levels[:, 0]

    def round_up(turn_index, current):
        top_field = march_up(current, adjoint, angles, sources, model_pair)
        return from_behind(top_field, "depth", -1)

    below = jnp.zeros((1, freq_count, tile_rows, full_width), jnp.float32)
    current = lax.fori_loop(0, depth_count - 1, round_up, below)
    upward = march_up(current, adjoint, angles, sources, model_pair)
    product = levels[:, 0] * levels[:, 1]
    picture = jnp.sum(product[..., :half_width] - product[..., half_width:], axis=1).reshape(
        step_count, tile_rows * half_width
    )
    surface_up = broadcast(upward[0], "depth", 0)
    row_share = tile_rows // depth_count
    row_start = depth_index * row_share
    own_part = lax.dynamic_slice_in_dim(surface_up, row_start, row_share, 1)
    own_seen = lax.dynamic_slice_in_dim(observed, row_start, row_share, 0)
    residual = jnp.transpose(own_part, (1, 0, 2)) - own_seen
    return (picture, residual)


def solution(mesh):
    in_specs = (
        P("shots", "lat", None),
        P(("shots", "lat"), None),
        P(("shots", "lat"), None),
        P(("shots", "lat")),
        P(),
        P(),
        P("depth", "lat"),
        P("depth", "lat"),
    )
    out_specs = (P(("shots", "depth"), "lat"), P(("shots", "lat", "depth"), None, None))
    return jax.shard_map(local, mesh=mesh, in_specs=in_specs, out_specs=out_specs, check_vma=False)
```

profile of v0, /device:TPU:0, one launch (start us, length us, event | category | flops | bytes accessed | tf_op | source)
XLA Modules:
  0.0 301.9 jit_solution(15912066643965686476)
XLA Ops:
  9.9 13.5 %all-reduce.8 = f32[32]{0:T(128)S(1)} all-reduce(f32[32]{0:T(128)S(1)} %fusion.48), channel_id=1, replica_groups=mesh['shots'=2,'lat'=4,'depth'=4] {'lat'}, use_global_device_ids=true, to_apply=%add.8 | all-reduce | flops 32 | bytes 256
  23.4 15.0 %all_gather.7 = f32[32,4096]{1,0:T(8,128)S(1)} all-gather(f32[8,4096]{1,0:T(8,128)} %param.13), channel_id=1, replica_groups=mesh['shots'=2,'lat'=4,'depth'=4] {'lat'}, dimensions={0}, use_global_device_ids=true | all-gather | bytes 655360 | tf_op jit(solution)/shard_map/all_gather | solution.py:100
  41.7 100.5 %while.28 = (s32[]{:T(128)}, f32[2,4,8,1024]{3,2,1,0:T(8,128)S(1)}, f32[4,2,9,9]{0,3,2,1:T(8,128)S(1)}, f32[2,4,8,1024]{3,2,1,0:T(8,128)S(1)}, f32[8,512]{1,0:T(8,128)S(1)}, /*index=5*/f32[4]{0:T(128)S(1)}, s32[]{:T(128)}) while((s32[]{:T(128)}, f32[2,4,8,1024]{3,2,1,0:T(8,128)S(1)}, f32[4,2,9,9]{0,3,2,1:T(8,128)S(1)}, ...), condition=%wide.region_1.2_spmd.clone.clone, body=%wide.region_0.1_spmd.clone.clone.sunk | while | flops 22265856 | bytes 10328341 | solution.py:119
  41.8 1.3 collective-permute-start
  43.1 4.6 %collective-permute-start.1 = (f32[2,4,4,1024]{3,2,1,0:T(4,128)S(1)}, f32[2,4,4,1024]{3,2,1,0:T(4,128)S(1)}, u32[]{:S(2)}, u32[]{:S(2)}) collective-permute-start(f32[2,4,4,1024]{3,2,1,0:T(4,128)S(1)} %get-tuple-element.1461), channel_id=1, source_target_pairs={{0,4},{4,8},{8,12},{1,5},{5,9},{9,13},{2,6},{6,10},{10,14},{3,7},{... | collective-permute-start | bytes 393224 | tf_op jit(solution)/shard_map/while/body/eval_jaxpr/ppermute | solution.py:16
  48.7 1.5 collective-permute-done.1
  50.3 18.9 %multiply_subtract_fusion.10 = (f32[2,4,8,512]{3,2,1,0:T(8,128)S(1)}, f32[2,4,8,512]{3,2,1,0:T(8,128)S(1)}, f32[2,4,8,512]{3,2,1,0:T(8,128)S(1)}) fusion(f32[4,8,512]{2,1,0:T(8,128)S(1)} %get-tuple-element.1360, f32[4,8,512]{2,1,0:T(8,128)S(1)} %get-tuple-element.1361, f32[4]{0:T(128)S(1)} %get-tuple-element.1362, f32[4]{0:T(128)S(1)} %get-tuple-element.1363, ...), kind=kLoop, calls=%fused_computation.173.clone.1 | loop fusion | flops 21757952 | bytes 2835456 | tf_op jit(solution)/shard_map/while/body/eval_jaxpr/sub | solution.py:45
  69.4 1.3 collective-permute-start.2
  71.9 1.3 collective-permute-start
  73.2 5.0 %collective-permute-start.1 = (f32[2,4,4,1024]{3,2,1,0:T(4,128)S(1)}, f32[2,4,4,1024]{3,2,1,0:T(4,128)S(1)}, u32[]{:S(2)}, u32[]{:S(2)}) collective-permute-start(f32[2,4,4,1024]{3,2,1,0:T(4,128)S(1)} %get-tuple-element.1461), channel_id=1, source_target_pairs={{0,4},{4,8},{8,12},{1,5},{5,9},{9,13},{2,6},{6,10},{10,14},{3,7},{... | collective-permute-start | bytes 393224 | tf_op jit(solution)/shard_map/while/body/eval_jaxpr/ppermute | solution.py:16
  79.2 1.5 collective-permute-done.1
  80.9 18.9 %multiply_subtract_fusion.10 = (f32[2,4,8,512]{3,2,1,0:T(8,128)S(1)}, f32[2,4,8,512]{3,2,1,0:T(8,128)S(1)}, f32[2,4,8,512]{3,2,1,0:T(8,128)S(1)}) fusion(f32[4,8,512]{2,1,0:T(8,128)S(1)} %get-tuple-element.1360, f32[4,8,512]{2,1,0:T(8,128)S(1)} %get-tuple-element.1361, f32[4]{0:T(128)S(1)} %get-tuple-element.1362, f32[4]{0:T(128)S(1)} %get-tuple-element.1363, ...), kind=kLoop, calls=%fused_computation.173.clone.1 | loop fusion | flops 21757952 | bytes 2835456 | tf_op jit(solution)/shard_map/while/body/eval_jaxpr/sub | solution.py:45
  99.9 5.4 %collective-permute-start.2 = (f32[2,4,8,1024]{3,2,1,0:T(8,128)S(1)}, f32[2,4,8,1024]{3,2,1,0:T(8,128)S(1)}, u32[]{:S(2)}, u32[]{:S(2)}) collective-permute-start(f32[2,4,8,1024]{3,2,1,0:T(8,128)S(1)} %pad_maximum_fusion.17), channel_id=1, source_target_pairs={{0,1},{1,2},{2,3},{4,5},{5,6},{6,7},{8,9},{9,10},{10,11},{12,13},{... | collective-permute-start | bytes 786440 | tf_op jit(solution)/shard_map/while/body/eval_jaxpr/ppermute | solution.py:25
  106.6 1.3 collective-permute-start
  107.9 4.7 %collective-permute-start.1 = (f32[2,4,4,1024]{3,2,1,0:T(4,128)S(1)}, f32[2,4,4,1024]{3,2,1,0:T(4,128)S(1)}, u32[]{:S(2)}, u32[]{:S(2)}) collective-permute-start(f32[2,4,4,1024]{3,2,1,0:T(4,128)S(1)} %get-tuple-element.1461), channel_id=1, source_target_pairs={{0,4},{4,8},{8,12},{1,5},{5,9},{9,13},{2,6},{6,10},{10,14},{3,7},{... | collective-permute-start | bytes 393224 | tf_op jit(solution)/shard_map/while/body/eval_jaxpr/ppermute | solution.py:16
  113.6 1.5 collective-permute-done.1
  115.2 18.9 %multiply_subtract_fusion.10 = (f32[2,4,8,512]{3,2,1,0:T(8,128)S(1)}, f32[2,4,8,512]{3,2,1,0:T(8,128)S(1)}, f32[2,4,8,512]{3,2,1,0:T(8,128)S(1)}) fusion(f32[4,8,512]{2,1,0:T(8,128)S(1)} %get-tuple-element.1360, f32[4,8,512]{2,1,0:T(8,128)S(1)} %get-tuple-element.1361, f32[4]{0:T(128)S(1)} %get-tuple-element.1362, f32[4]{0:T(128)S(1)} %get-tuple-element.1363, ...), kind=kLoop, calls=%fused_computation.173.clone.1 | loop fusion | flops 21757952 | bytes 2835456 | tf_op jit(solution)/shard_map/while/body/eval_jaxpr/sub | solution.py:45
  134.3 6.9 %collective-permute-start.2 = (f32[2,4,8,1024]{3,2,1,0:T(8,128)S(1)}, f32[2,4,8,1024]{3,2,1,0:T(8,128)S(1)}, u32[]{:S(2)}, u32[]{:S(2)}) collective-permute-start(f32[2,4,8,1024]{3,2,1,0:T(8,128)S(1)} %pad_maximum_fusion.17), channel_id=1, source_target_pairs={{0,1},{1,2},{2,3},{4,5},{5,6},{6,7},{8,9},{9,10},{10,11},{12,13},{... | collective-permute-start | bytes 786440 | tf_op jit(solution)/shard_map/while/body/eval_jaxpr/ppermute | solution.py:25
  142.3 4.1 %collective-permute-start.6 = (f32[2,4,4,1024]{3,2,1,0:T(4,128)S(1)}, f32[2,4,4,1024]{3,2,1,0:T(4,128)S(1)}, u32[]{:S(2)}, u32[]{:S(2)}) collective-permute-start(f32[2,4,4,1024]{3,2,1,0:T(4,128)S(1)} %get-tuple-element.844), channel_id=1, source_target_pairs={{0,4},{4,8},{8,12},{1,5},{5,9},{9,13},{2,6},{6,10},{10,14},{3,7},{... | collective-permute-start | bytes 393224 | tf_op jit(solution)/shard_map/ppermute | solution.py:16
  146.4 1.3 collective-permute-start.7
  151.7 1.6 collective-permute-done.7
  153.5 19.0 %multiply_subtract_fusion.3 = (f32[2,4,8,512]{3,2,1,0:T(8,128)S(1)}, f32[2,4,8,512]{3,2,1,0:T(8,128)S(1)}, f32[2,4,8,512]{3,2,1,0:T(8,128)S(1)}) fusion(f32[4,8,512]{2,1,0:T(8,128)S(1)} %get-tuple-element.938, f32[4,8,512]{2,1,0:T(8,128)S(1)} %get-tuple-element.937, f32[4]{0:T(128)S(1)} %get-tuple-element.426, f32[4]{0:T(128)S(1)} %get-tuple-element.425, ...), kind=kLoop, calls=%fused_computation.1000 | loop fusion | flops 21757952 | bytes 2835456 | tf_op jit(solution)/shard_map/sub | solution.py:45
  172.5 72.3 %while.29 = (s32[]{:T(128)}, f32[1,4,8,1024]{3,2,1,0:T(8,128)S(1)}, f32[4,1,9,9]{0,3,2,1:T(8,128)S(1)}, f32[1,8,1024]{2,1,0:T(8,128)S(1)}, f32[1,4,8,1024]{3,2,1...) while((s32[]{:T(128)}, f32[1,4,8,1024]{3,2,1,0:T(8,128)S(1)}, ...), condition=%wide.region_4.5_spmd.clone.clone, body=%wide.region_3.4_spmd.clone.clone.sunk | while | flops 11239426 | bytes 7006565 | solution.py:128
  172.9 3.9 %collective-permute-start.3 = (f32[1,4,4,1024]{3,2,1,0:T(4,128)S(1)}, f32[1,4,4,1024]{3,2,1,0:T(4,128)S(1)}, u32[]{:S(2)}, u32[]{:S(2)}) collective-permute-start(f32[1,4,4,1024]{3,2,1,0:T(4,128)S(1)} %get-tuple-element.1541), channel_id=1, source_target_pairs={{0,4},{4,8},{8,12},{1,5},{5,9},{9,13},{2,6},{6,10},{10,14},{3,7},{... | collective-permute-start | bytes 196616 | tf_op jit(solution)/shard_map/while/body/eval_jaxpr/ppermute | solution.py:16
  176.9 1.3 collective-permute-start.4
  178.7 4.3 %collective-permute-done.4 = f32[1,4,4,1024]{3,2,1,0:T(4,128)S(1)} collective-permute-done((f32[1,4,4,1024]{3,2,1,0:T(4,128)S(1)}, f32[1,4,4,1024]{3,2,1,0:T(4,128)S(1)}, u32[]{:S(2)}, u32[]{:S(2)}) %collective-permute-start.4) | collective-permute-done | bytes 65568 | tf_op jit(solution)/shard_map/while/body/eval_jaxpr/ppermute | solution.py:17
  183.2 3.7 %multiply_subtract_fusion.11 = f32[1,4,8,512]{3,2,1,0:T(8,128)S(1)} fusion(f32[1,4,8,512]{3,2,1,0:T(8,128)S(1)} %get-tuple-element.1539, f32[1,4,8,512]{3,2,1,0:T(8,128)S(1)} %get-tuple-element.1540, f32[1,4,12,1024]{3,2,1,0:T(8,128)S(1)} %get-tuple-element.1543, f32[1,4,12,1024]{3,2,1,0:T(8,128)S(1)} %get-tuple-element.1544, ...), kind=kLoop, calls=%fused_computation.510.clone.1 | loop fusion | flops 5292032 | bytes 1509920 | tf_op jit(solution)/shard_map/while/body/eval_jaxpr/sub | solution.py:72
  186.8 3.7 %multiply_add_fusion.21 = f32[1,4,8,512]{3,2,1,0:T(8,128)S(1)} fusion(f32[1,4,8,512]{3,2,1,0:T(8,128)S(1)} %get-tuple-element.1539, f32[1,4,8,512]{3,2,1,0:T(8,128)S(1)} %get-tuple-element.1540, f32[1,4,12,1024]{3,2,1,0:T(8,128)S(1)} %get-tuple-element.1543, f32[1,4,12,1024]{3,2,1,0:T(8,128)S(1)} %get-tuple-element.1544, ...), kind=kLoop, calls=%fused_computation.508.clone.1 | loop fusion | flops 5292032 | bytes 1509920 | tf_op jit(solution)/shard_map/while/body/eval_jaxpr/add | solution.py:73
  190.5 1.3 collective-permute-start.5
  191.8 4.9 %collective-permute-done.5 = f32[1,4,8,1024]{3,2,1,0:T(8,128)S(1)} collective-permute-done((f32[1,4,8,1024]{3,2,1,0:T(8,128)S(1)}, f32[1,4,8,1024]{3,2,1,0:T(8,128)S(1)}, u32[]{:S(2)}, u32[]{:S(2)}) %collective-permute-start.5) | collective-permute-done | bytes 131104 | tf_op jit(solution)/shard_map/while/body/eval_jaxpr/ppermute | solution.py:25
  197.1 3.6 %collective-permute-start.3 = (f32[1,4,4,1024]{3,2,1,0:T(4,128)S(1)}, f32[1,4,4,1024]{3,2,1,0:T(4,128)S(1)}, u32[]{:S(2)}, u32[]{:S(2)}) collective-permute-start(f32[1,4,4,1024]{3,2,1,0:T(4,128)S(1)} %get-tuple-element.1541), channel_id=1, source_target_pairs={{0,4},{4,8},{8,12},{1,5},{5,9},{9,13},{2,6},{6,10},{10,14},{3,7},{... | collective-permute-start | bytes 196616 | tf_op jit(solution)/shard_map/while/body/eval_jaxpr/ppermute | solution.py:16
  200.7 1.3 collective-permute-start.4
  202.6 4.3 %collective-permute-done.4 = f32[1,4,4,1024]{3,2,1,0:T(4,128)S(1)} collective-permute-done((f32[1,4,4,1024]{3,2,1,0:T(4,128)S(1)}, f32[1,4,4,1024]{3,2,1,0:T(4,128)S(1)}, u32[]{:S(2)}, u32[]{:S(2)}) %collective-permute-start.4) | collective-permute-done | bytes 65568 | tf_op jit(solution)/shard_map/while/body/eval_jaxpr/ppermute | solution.py:17
  207.0 3.7 %multiply_subtract_fusion.11 = f32[1,4,8,512]{3,2,1,0:T(8,128)S(1)} fusion(f32[1,4,8,512]{3,2,1,0:T(8,128)S(1)} %get-tuple-element.1539, f32[1,4,8,512]{3,2,1,0:T(8,128)S(1)} %get-tuple-element.1540, f32[1,4,12,1024]{3,2,1,0:T(8,128)S(1)} %get-tuple-element.1543, f32[1,4,12,1024]{3,2,1,0:T(8,128)S(1)} %get-tuple-element.1544, ...), kind=kLoop, calls=%fused_computation.510.clone.1 | loop fusion | flops 5292032 | bytes 1509920 | tf_op jit(solution)/shard_map/while/body/eval_jaxpr/sub | solution.py:72
  210.7 3.7 %multiply_add_fusion.21 = f32[1,4,8,512]{3,2,1,0:T(8,128)S(1)} fusion(f32[1,4,8,512]{3,2,1,0:T(8,128)S(1)} %get-tuple-element.1539, f32[1,4,8,512]{3,2,1,0:T(8,128)S(1)} %get-tuple-element.1540, f32[1,4,12,1024]{3,2,1,0:T(8,128)S(1)} %get-tuple-element.1543, f32[1,4,12,1024]{3,2,1,0:T(8,128)S(1)} %get-tuple-element.1544, ...), kind=kLoop, calls=%fused_computation.508.clone.1 | loop fusion | flops 5292032 | bytes 1509920 | tf_op jit(solution)/shard_map/while/body/eval_jaxpr/add | solution.py:73
  214.4 1.3 collective-permute-start.5
  215.7 6.9 %collective-permute-done.5 = f32[1,4,8,1024]{3,2,1,0:T(8,128)S(1)} collective-permute-done((f32[1,4,8,1024]{3,2,1,0:T(8,128)S(1)}, f32[1,4,8,1024]{3,2,1,0:T(8,128)S(1)}, u32[]{:S(2)}, u32[]{:S(2)}) %collective-permute-start.5) | collective-permute-done | bytes 131104 | tf_op jit(solution)/shard_map/while/body/eval_jaxpr/ppermute | solution.py:25
  223.0 3.3 %collective-permute-start.3 = (f32[1,4,4,1024]{3,2,1,0:T(4,128)S(1)}, f32[1,4,4,1024]{3,2,1,0:T(4,128)S(1)}, u32[]{:S(2)}, u32[]{:S(2)}) collective-permute-start(f32[1,4,4,1024]{3,2,1,0:T(4,128)S(1)} %get-tuple-element.1541), channel_id=1, source_target_pairs={{0,4},{4,8},{8,12},{1,5},{5,9},{9,13},{2,6},{6,10},{10,14},{3,7},{... | collective-permute-start | bytes 196616 | tf_op jit(solution)/shard_map/while/body/eval_jaxpr/ppermute | solution.py:16
  226.3 1.3 collective-permute-start.4
  228.2 4.3 %collective-permute-done.4 = f32[1,4,4,1024]{3,2,1,0:T(4,128)S(1)} collective-permute-done((f32[1,4,4,1024]{3,2,1,0:T(4,128)S(1)}, f32[1,4,4,1024]{3,2,1,0:T(4,128)S(1)}, u32[]{:S(2)}, u32[]{:S(2)}) %collective-permute-start.4) | collective-permute-done | bytes 65568 | tf_op jit(solution)/shard_map/while/body/eval_jaxpr/ppermute | solution.py:17
  232.6 3.7 %multiply_subtract_fusion.11 = f32[1,4,8,512]{3,2,1,0:T(8,128)S(1)} fusion(f32[1,4,8,512]{3,2,1,0:T(8,128)S(1)} %get-tuple-element.1539, f32[1,4,8,512]{3,2,1,0:T(8,128)S(1)} %get-tuple-element.1540, f32[1,4,12,1024]{3,2,1,0:T(8,128)S(1)} %get-tuple-element.1543, f32[1,4,12,1024]{3,2,1,0:T(8,128)S(1)} %get-tuple-element.1544, ...), kind=kLoop, calls=%fused_computation.510.clone.1 | loop fusion | flops 5292032 | bytes 1509920 | tf_op jit(solution)/shard_map/while/body/eval_jaxpr/sub | solution.py:72
  236.3 3.7 %multiply_add_fusion.21 = f32[1,4,8,512]{3,2,1,0:T(8,128)S(1)} fusion(f32[1,4,8,512]{3,2,1,0:T(8,128)S(1)} %get-tuple-element.1539, f32[1,4,8,512]{3,2,1,0:T(8,128)S(1)} %get-tuple-element.1540, f32[1,4,12,1024]{3,2,1,0:T(8,128)S(1)} %get-tuple-element.1543, f32[1,4,12,1024]{3,2,1,0:T(8,128)S(1)} %get-tuple-element.1544, ...), kind=kLoop, calls=%fused_computation.508.clone.1 | loop fusion | flops 5292032 | bytes 1509920 | tf_op jit(solution)/shard_map/while/body/eval_jaxpr/add | solution.py:73
  241.2 3.6 %collective-permute-done.5 = f32[1,4,8,1024]{3,2,1,0:T(8,128)S(1)} collective-permute-done((f32[1,4,8,1024]{3,2,1,0:T(8,128)S(1)}, f32[1,4,8,1024]{3,2,1,0:T(8,128)S(1)}, u32[]{:S(2)}, u32[]{:S(2)}) %collective-permute-start.5) | collective-permute-done | bytes 131104 | tf_op jit(solution)/shard_map/while/body/eval_jaxpr/ppermute | solution.py:25
  245.2 2.4 collective-permute-start.8
  249.3 4.5 %collective-permute-done.9 = f32[1,4,4,1024]{3,2,1,0:T(4,128)S(1)} collective-permute-done((f32[1,4,4,1024]{3,2,1,0:T(4,128)S(1)}, f32[1,4,4,1024]{3,2,1,0:T(4,128)S(1)}, u32[]{:S(2)}, u32[]{:S(2)}) %collective-permute-start.9) | collective-permute-done | bytes 65568 | tf_op jit(solution)/shard_map/ppermute | solution.py:17
  253.9 3.7 %multiply_subtract_fusion.5 = f32[1,4,8,512]{3,2,1,0:T(8,128)S(1)} fusion(f32[1,4,8,512]{3,2,1,0:T(8,128)S(1)} %get-tuple-element.847, f32[1,4,8,512]{3,2,1,0:T(8,128)S(1)} %get-tuple-element.846, f32[1,4,12,1024]{3,2,1,0:T(8,128)S(1)} %get-tuple-element.851, f32[1,4,12,1024]{3,2,1,0:T(8,128)S(1)} %get-tuple-element.850, ...), kind=kLoop, calls=%fused_computation.1023 | loop fusion | flops 5292032 | bytes 1509920 | tf_op jit(solution)/shard_map/sub | solution.py:72
  257.5 3.7 %multiply_add_fusion.13 = f32[1,4,8,512]{3,2,1,0:T(8,128)S(1)} fusion(f32[1,4,8,512]{3,2,1,0:T(8,128)S(1)} %get-tuple-element.847, f32[1,4,8,512]{3,2,1,0:T(8,128)S(1)} %get-tuple-element.846, f32[1,4,12,1024]{3,2,1,0:T(8,128)S(1)} %get-tuple-element.851, f32[1,4,12,1024]{3,2,1,0:T(8,128)S(1)} %get-tuple-element.850, ...), kind=kLoop, calls=%fused_computation.1021 | loop fusion | flops 5292032 | bytes 1509920 | tf_op jit(solution)/shard_map/add | solution.py:73
  262.5 30.9 %all-reduce.11.cloned.1.call-done = f32[4,8,1024]{2,1,0:T(8,128)} async-done(((f32[4,8,1024]{2,1,0:T(8,128)}), f32[4,8,1024]{2,1,0:T(8,128)}) %all-reduce.11.cloned.1.call-update) | async-done | bytes 131088 | tf_op jit(solution)/shard_map/psum | solution.py:30
  (187 shorter events, 25.9 us)
Async XLA Ops:
  7.2 286.3 %all-reduce.11.cloned.1.call-start = ((), (), s32[]{:S(2)}) async-start(), calls=%async_computation | async-start | bytes 262144 | tf_op jit(solution)/shard_map/psum | solution.py:30
  7.2 0.7 copy-start.7
  9.1 0.7 copy-start.5
  9.1 0.7 copy-start.6
  38.7 0.9 copy-start.1
  39.7 0.7 copy-start.4
  39.7 1.4 copy-start
  41.1 0.7 copy-start.2
  41.8 6.9 %collective-permute-start = (f32[2,4,4,1024]{3,2,1,0:T(4,128)S(1)}, f32[2,4,4,1024]{3,2,1,0:T(4,128)S(1)}, u32[]{:S(2)}, u32[]{:S(2)}) collective-permute-start(f32[2,4,4,1024]{3,2,1,0:T(4,128)S(1)} %get-tuple-element.1370), channel_id=1, source_target_pairs={{4,0},{8,4},{12,8},{5,1},{9,5},{13,9},{6,2},{10,6},{14,10},{7,3},{... | collective-permute-start | bytes 393224 | tf_op jit(solution)/shard_map/while/body/eval_jaxpr/ppermute | solution.py:17
  43.1 7.1 %collective-permute-start.1 = (f32[2,4,4,1024]{3,2,1,0:T(4,128)S(1)}, f32[2,4,4,1024]{3,2,1,0:T(4,128)S(1)}, u32[]{:S(2)}, u32[]{:S(2)}) collective-permute-start(f32[2,4,4,1024]{3,2,1,0:T(4,128)S(1)} %get-tuple-element.1461), channel_id=1, source_target_pairs={{0,4},{4,8},{8,12},{1,5},{5,9},{9,13},{2,6},{6,10},{10,14},{3,7},{... | collective-permute-start | bytes 393224 | tf_op jit(solution)/shard_map/while/body/eval_jaxpr/ppermute | solution.py:16
  69.4 2.4 collective-permute-start.2
  71.9 7.3 %collective-permute-start = (f32[2,4,4,1024]{3,2,1,0:T(4,128)S(1)}, f32[2,4,4,1024]{3,2,1,0:T(4,128)S(1)}, u32[]{:S(2)}, u32[]{:S(2)}) collective-permute-start(f32[2,4,4,1024]{3,2,1,0:T(4,128)S(1)} %get-tuple-element.1370), channel_id=1, source_target_pairs={{4,0},{8,4},{12,8},{5,1},{9,5},{13,9},{6,2},{10,6},{14,10},{7,3},{... | collective-permute-start | bytes 393224 | tf_op jit(solution)/shard_map/while/body/eval_jaxpr/ppermute | solution.py:17
  73.2 7.5 %collective-permute-start.1 = (f32[2,4,4,1024]{3,2,1,0:T(4,128)S(1)}, f32[2,4,4,1024]{3,2,1,0:T(4,128)S(1)}, u32[]{:S(2)}, u32[]{:S(2)}) collective-permute-start(f32[2,4,4,1024]{3,2,1,0:T(4,128)S(1)} %get-tuple-element.1461), channel_id=1, source_target_pairs={{0,4},{4,8},{8,12},{1,5},{5,9},{9,13},{2,6},{6,10},{10,14},{3,7},{... | collective-permute-start | bytes 393224 | tf_op jit(solution)/shard_map/while/body/eval_jaxpr/ppermute | solution.py:16
  99.9 6.6 %collective-permute-start.2 = (f32[2,4,8,1024]{3,2,1,0:T(8,128)S(1)}, f32[2,4,8,1024]{3,2,1,0:T(8,128)S(1)}, u32[]{:S(2)}, u32[]{:S(2)}) collective-permute-start(f32[2,4,8,1024]{3,2,1,0:T(8,128)S(1)} %pad_maximum_fusion.17), channel_id=1, source_target_pairs={{0,1},{1,2},{2,3},{4,5},{5,6},{6,7},{8,9},{9,10},{10,11},{12,13},{... | collective-permute-start | bytes 786440 | tf_op jit(solution)/shard_map/while/body/eval_jaxpr/ppermute | solution.py:25
  106.6 7.0 %collective-permute-start = (f32[2,4,4,1024]{3,2,1,0:T(4,128)S(1)}, f32[2,4,4,1024]{3,2,1,0:T(4,128)S(1)}, u32[]{:S(2)}, u32[]{:S(2)}) collective-permute-start(f32[2,4,4,1024]{3,2,1,0:T(4,128)S(1)} %get-tuple-element.1370), channel_id=1, source_target_pairs={{4,0},{8,4},{12,8},{5,1},{9,5},{13,9},{6,2},{10,6},{14,10},{7,3},{... | collective-permute-start | bytes 393224 | tf_op jit(solution)/shard_map/while/body/eval_jaxpr/ppermute | solution.py:17
  107.9 7.2 %collective-permute-start.1 = (f32[2,4,4,1024]{3,2,1,0:T(4,128)S(1)}, f32[2,4,4,1024]{3,2,1,0:T(4,128)S(1)}, u32[]{:S(2)}, u32[]{:S(2)}) collective-permute-start(f32[2,4,4,1024]{3,2,1,0:T(4,128)S(1)} %get-tuple-element.1461), channel_id=1, source_target_pairs={{0,4},{4,8},{8,12},{1,5},{5,9},{9,13},{2,6},{6,10},{10,14},{3,7},{... | collective-permute-start | bytes 393224 | tf_op jit(solution)/shard_map/while/body/eval_jaxpr/ppermute | solution.py:16
  134.3 8.0 %collective-permute-start.2 = (f32[2,4,8,1024]{3,2,1,0:T(8,128)S(1)}, f32[2,4,8,1024]{3,2,1,0:T(8,128)S(1)}, u32[]{:S(2)}, u32[]{:S(2)}) collective-permute-start(f32[2,4,8,1024]{3,2,1,0:T(8,128)S(1)} %pad_maximum_fusion.17), channel_id=1, source_target_pairs={{0,1},{1,2},{2,3},{4,5},{5,6},{6,7},{8,9},{9,10},{10,11},{12,13},{... | collective-permute-start | bytes 786440 | tf_op jit(solution)/shard_map/while/body/eval_jaxpr/ppermute | solution.py:25
  142.3 9.4 %collective-permute-start.6 = (f32[2,4,4,1024]{3,2,1,0:T(4,128)S(1)}, f32[2,4,4,1024]{3,2,1,0:T(4,128)S(1)}, u32[]{:S(2)}, u32[]{:S(2)}) collective-permute-start(f32[2,4,4,1024]{3,2,1,0:T(4,128)S(1)} %get-tuple-element.844), channel_id=1, source_target_pairs={{0,4},{4,8},{8,12},{1,5},{5,9},{9,13},{2,6},{6,10},{10,14},{3,7},{... | collective-permute-start | bytes 393224 | tf_op jit(solution)/shard_map/ppermute | solution.py:16
  146.4 6.9 %collective-permute-start.7 = (f32[2,4,4,1024]{3,2,1,0:T(4,128)S(1)}, f32[2,4,4,1024]{3,2,1,0:T(4,128)S(1)}, u32[]{:S(2)}, u32[]{:S(2)}) collective-permute-start(f32[2,4,4,1024]{3,2,1,0:T(4,128)S(1)} %get-tuple-element.845), channel_id=1, source_target_pairs={{4,0},{8,4},{12,8},{5,1},{9,5},{13,9},{6,2},{10,6},{14,10},{7,3},{... | collective-permute-start | bytes 393224 | tf_op jit(solution)/shard_map/ppermute | solution.py:17
  150.7 0.7 copy-start.3
  172.9 5.8 %collective-permute-start.3 = (f32[1,4,4,1024]{3,2,1,0:T(4,128)S(1)}, f32[1,4,4,1024]{3,2,1,0:T(4,128)S(1)}, u32[]{:S(2)}, u32[]{:S(2)}) collective-permute-start(f32[1,4,4,1024]{3,2,1,0:T(4,128)S(1)} %get-tuple-element.1541), channel_id=1, source_target_pairs={{0,4},{4,8},{8,12},{1,5},{5,9},{9,13},{2,6},{6,10},{10,14},{3,7},{... | collective-permute-start | bytes 196616 | tf_op jit(solution)/shard_map/while/body/eval_jaxpr/ppermute | solution.py:16
  176.9 6.2 %collective-permute-start.4 = (f32[1,4,4,1024]{3,2,1,0:T(4,128)S(1)}, f32[1,4,4,1024]{3,2,1,0:T(4,128)S(1)}, u32[]{:S(2)}, u32[]{:S(2)}) collective-permute-start(f32[1,4,4,1024]{3,2,1,0:T(4,128)S(1)} %get-tuple-element.1542), channel_id=1, source_target_pairs={{4,0},{8,4},{12,8},{5,1},{9,5},{13,9},{6,2},{10,6},{14,10},{7,3},{... | collective-permute-start | bytes 196616 | tf_op jit(solution)/shard_map/while/body/eval_jaxpr/ppermute | solution.py:17
  190.5 6.2 %collective-permute-start.5 = (f32[1,4,8,1024]{3,2,1,0:T(8,128)S(1)}, f32[1,4,8,1024]{3,2,1,0:T(8,128)S(1)}, u32[]{:S(2)}, u32[]{:S(2)}) collective-permute-start(f32[1,4,8,1024]{3,2,1,0:T(8,128)S(1)} %pad_maximum_fusion.19), channel_id=1, source_target_pairs={{1,0},{2,1},{3,2},{5,4},{6,5},{7,6},{9,8},{10,9},{11,10},{13,12},{... | collective-permute-start | bytes 393224 | tf_op jit(solution)/shard_map/while/body/eval_jaxpr/ppermute | solution.py:25
  197.1 5.5 %collective-permute-start.3 = (f32[1,4,4,1024]{3,2,1,0:T(4,128)S(1)}, f32[1,4,4,1024]{3,2,1,0:T(4,128)S(1)}, u32[]{:S(2)}, u32[]{:S(2)}) collective-permute-start(f32[1,4,4,1024]{3,2,1,0:T(4,128)S(1)} %get-tuple-element.1541), channel_id=1, source_target_pairs={{0,4},{4,8},{8,12},{1,5},{5,9},{9,13},{2,6},{6,10},{10,14},{3,7},{... | collective-permute-start | bytes 196616 | tf_op jit(solution)/shard_map/while/body/eval_jaxpr/ppermute | solution.py:16
  200.7 6.2 %collective-permute-start.4 = (f32[1,4,4,1024]{3,2,1,0:T(4,128)S(1)}, f32[1,4,4,1024]{3,2,1,0:T(4,128)S(1)}, u32[]{:S(2)}, u32[]{:S(2)}) collective-permute-start(f32[1,4,4,1024]{3,2,1,0:T(4,128)S(1)} %get-tuple-element.1542), channel_id=1, source_target_pairs={{4,0},{8,4},{12,8},{5,1},{9,5},{13,9},{6,2},{10,6},{14,10},{7,3},{... | collective-permute-start | bytes 196616 | tf_op jit(solution)/shard_map/while/body/eval_jaxpr/ppermute | solution.py:17
  214.4 8.2 %collective-permute-start.5 = (f32[1,4,8,1024]{3,2,1,0:T(8,128)S(1)}, f32[1,4,8,1024]{3,2,1,0:T(8,128)S(1)}, u32[]{:S(2)}, u32[]{:S(2)}) collective-permute-start(f32[1,4,8,1024]{3,2,1,0:T(8,128)S(1)} %pad_maximum_fusion.19), channel_id=1, source_target_pairs={{1,0},{2,1},{3,2},{5,4},{6,5},{7,6},{9,8},{10,9},{11,10},{13,12},{... | collective-permute-start | bytes 393224 | tf_op jit(solution)/shard_map/while/body/eval_jaxpr/ppermute | solution.py:25
  223.0 5.2 %collective-permute-start.3 = (f32[1,4,4,1024]{3,2,1,0:T(4,128)S(1)}, f32[1,4,4,1024]{3,2,1,0:T(4,128)S(1)}, u32[]{:S(2)}, u32[]{:S(2)}) collective-permute-start(f32[1,4,4,1024]{3,2,1,0:T(4,128)S(1)} %get-tuple-element.1541), channel_id=1, source_target_pairs={{0,4},{4,8},{8,12},{1,5},{5,9},{9,13},{2,6},{6,10},{10,14},{3,7},{... | collective-permute-start | bytes 196616 | tf_op jit(solution)/shard_map/while/body/eval_jaxpr/ppermute | solution.py:16
  226.3 6.2 %collective-permute-start.4 = (f32[1,4,4,1024]{3,2,1,0:T(4,128)S(1)}, f32[1,4,4,1024]{3,2,1,0:T(4,128)S(1)}, u32[]{:S(2)}, u32[]{:S(2)}) collective-permute-start(f32[1,4,4,1024]{3,2,1,0:T(4,128)S(1)} %get-tuple-element.1542), channel_id=1, source_target_pairs={{4,0},{8,4},{12,8},{5,1},{9,5},{13,9},{6,2},{10,6},{14,10},{7,3},{... | collective-permute-start | bytes 196616 | tf_op jit(solution)/shard_map/while/body/eval_jaxpr/ppermute | solution.py:17
  239.9 4.9 %collective-permute-start.5 = (f32[1,4,8,1024]{3,2,1,0:T(8,128)S(1)}, f32[1,4,8,1024]{3,2,1,0:T(8,128)S(1)}, u32[]{:S(2)}, u32[]{:S(2)}) collective-permute-start(f32[1,4,8,1024]{3,2,1,0:T(8,128)S(1)} %pad_maximum_fusion.19), channel_id=1, source_target_pairs={{1,0},{2,1},{3,2},{5,4},{6,5},{7,6},{9,8},{10,9},{11,10},{13,12},{... | collective-permute-start | bytes 393224 | tf_op jit(solution)/shard_map/while/body/eval_jaxpr/ppermute | solution.py:25
  245.2 4.1 %collective-permute-start.8 = (f32[1,4,4,1024]{3,2,1,0:T(4,128)S(1)}, f32[1,4,4,1024]{3,2,1,0:T(4,128)S(1)}, u32[]{:S(2)}, u32[]{:S(2)}) collective-permute-start(f32[1,4,4,1024]{3,2,1,0:T(4,128)S(1)} %get-tuple-element.852), channel_id=1, source_target_pairs={{0,4},{4,8},{8,12},{1,5},{5,9},{9,13},{2,6},{6,10},{10,14},{3,7},{... | collective-permute-start | bytes 196616 | tf_op jit(solution)/shard_map/ppermute | solution.py:16
  247.6 6.2 %collective-permute-start.9 = (f32[1,4,4,1024]{3,2,1,0:T(4,128)S(1)}, f32[1,4,4,1024]{3,2,1,0:T(4,128)S(1)}, u32[]{:S(2)}, u32[]{:S(2)}) collective-permute-start(f32[1,4,4,1024]{3,2,1,0:T(4,128)S(1)} %get-tuple-element.853), channel_id=1, source_target_pairs={{4,0},{8,4},{12,8},{5,1},{9,5},{13,9},{6,2},{10,6},{14,10},{7,3},{... | collective-permute-start | bytes 196616 | tf_op jit(solution)/shard_map/ppermute | solution.py:17
Sparse Core Ops, SparseCore 0:
  262.0 31.4 all-reduce.10
where the time goes:
time: 303 us; the launch traced here: 302 us
  other arithmetic  111 us (37%)
  waiting for transfers between devices  76.1 us (25%)
  starting transfers between devices  59.4 us (20%)
  blocking collectives  28.5 us (9%)
  between operations  15.1 us (5%)
  local copies, waits for them, and re-layouts  10.2 us (3%)
    sub x8, other arithmetic, rotate(): real_part * cosine - imag_part * sine_part  77.1 us
    ppermute x8, starting transfers between devices, padded_2(): before = lax.ppermute(last, axis, up)  31.5 us
    psum x1, waiting for transfers between devices, broadcast(): return lax.psum(block, axis)  30.9 us
    ppermute x8, waiting for transfers between devices, padded_2(): after = lax.ppermute(leading, axis, down)  20.3 us
    ppermute x6, waiting for transfers between devices, from_behind(): lax.ppermute(value, axis, [(source, source + steps) for source in range(l...  18.7 us
    ppermute x6, starting transfers between devices, from_behind(): lax.ppermute(value, axis, [(source, source + steps) for source in range(l...  17.5 us
    all_gather x1, blocking collectives, local(): piece_traces = lax.all_gather(traces, 'lat', axis=0, tiled=True)  15 us
    add x4, other arithmetic, convolve(): out_imag = out_imag + tap_imag * real_piece + tap_real * imag_piece  14.6 us
  transfers between devices with their start and end apart: 23, of which 22 were waited for; matrix products, arithmetic and copies ran while one was open for 2% of the time, Pallas kernels for 0%

commit v1 on v0

--- a/solution.py
+++ b/solution.py
@@ -27,7 +27,7 @@
 
 def broadcast(block, axis, holder):
     block = jnp.where(lax.axis_index(axis) == holder, block, jnp.zeros_like(block))
-    return lax.psum(block, axis)
+    return jnp.sum(lax.all_gather(block, axis), axis=0)
 
 
 def make_taps(stencil):

time: 303 us -> 265 us (0.87)
  waiting for transfers between devices: 76.1 us -> 44.3 us
  between operations: 15.1 us -> 1.71 us
  blocking collectives: 28.5 us -> 37.6 us
    psum x1 -> x0, waiting for transfers between devices: 30.9 us -> none  [broadcast(): return lax.psum(block, axis)]
    all_gather x0 -> x1, blocking collectives: none -> 9.06 us  [broadcast(): return jnp.sum(lax.all_gather(block, axis), axis=0)]
  transfers between devices with their start and end apart: 23 -> 22, of which waited for: 22 -> 20; matrix products, arithmetic and copies ran while one was open for 2% -> 2% of each run, Pallas kernels for 0% -> 0%
where the time goes in v1:
time: 265 us; the launch traced here: 264 us
  other arithmetic  110 us (42%)
  starting transfers between devices  59.4 us (22%)
  waiting for transfers between devices  44.3 us (17%)
  blocking collectives  37.6 us (14%)
  local copies, waits for them, and re-layouts  10.2 us (4%)
    sub x8, other arithmetic, rotate(): real_part * cosine - imag_part * sine_part  77.1 us
    ppermute x8, starting transfers between devices, padded_2(): before = lax.ppermute(last, axis, up)  31.4 us
    ppermute x8, waiting for transfers between devices, padded_2(): after = lax.ppermute(leading, axis, down)  19.8 us
    ppermute x6, waiting for transfers between devices, from_behind(): lax.ppermute(value, axis, [(source, source + steps) for source in range(l...  18.7 us
    ppermute x6, starting transfers between devices, from_behind(): lax.ppermute(value, axis, [(source, source + steps) for source in range(l...  17.5 us
    all_gather x1, blocking collectives, local(): piece_traces = lax.all_gather(traces, 'lat', axis=0, tiled=True)  15 us
    add x4, other arithmetic, convolve(): out_imag = out_imag + tap_imag * real_piece + tap_real * imag_piece  14.6 us
    sub x4, other arithmetic, convolve(): out_real = out_real + tap_real * real_piece - tap_imag * imag_piece  14.6 us
  transfers between devices with their start and end apart: 22, of which 20 were waited for; matrix products, arithmetic and copies ran while one was open for 2% of the time, Pallas kernels for 0%

profile of v1, /device:TPU:0, one launch (start us, length us, event | category | flops | bytes accessed | tf_op | source)
XLA Modules:
  0.0 264.2 jit_solution(6957278127998083286)
XLA Ops:
  3.3 13.5 %all-reduce.8 = f32[32]{0:T(128)S(1)} all-reduce(f32[32]{0:T(128)S(1)} %fusion.47), channel_id=1, replica_groups=mesh['shots'=2,'lat'=4,'depth'=4] {'lat'}, use_global_device_ids=true, to_apply=%add.8 | all-reduce | flops 32 | bytes 256
  16.8 15.0 %all_gather.11 = f32[32,4096]{1,0:T(8,128)S(1)} all-gather(f32[8,4096]{1,0:T(8,128)} %param.13), channel_id=1, replica_groups=mesh['shots'=2,'lat'=4,'depth'=4] {'lat'}, dimensions={0}, use_global_device_ids=true | all-gather | bytes 655360 | tf_op jit(solution)/shard_map/all_gather | solution.py:100
  35.2 100.5 %while.28 = (s32[]{:T(128)}, f32[2,4,8,1024]{3,2,1,0:T(8,128)S(1)}, f32[4,2,9,9]{0,3,2,1:T(8,128)S(1)}, f32[2,4,8,1024]{3,2,1,0:T(8,128)S(1)}, f32[8,512]{1,0:T(8,128)S(1)}, /*index=5*/f32[4]{0:T(128)S(1)}, s32[]{:T(128)}) while((s32[]{:T(128)}, f32[2,4,8,1024]{3,2,1,0:T(8,128)S(1)}, f32[4,2,9,9]{0,3,2,1:T(8,128)S(1)}, ...), condition=%wide.region_1.2_spmd.clone.clone, body=%wide.region_0.1_spmd.clone.clone.sunk | while | flops 22265856 | bytes 10328341 | solution.py:119
  35.2 1.3 collective-permute-start
  36.5 4.6 %collective-permute-start.1 = (f32[2,4,4,1024]{3,2,1,0:T(4,128)S(1)}, f32[2,4,4,1024]{3,2,1,0:T(4,128)S(1)}, u32[]{:S(2)}, u32[]{:S(2)}) collective-permute-start(f32[2,4,4,1024]{3,2,1,0:T(4,128)S(1)} %get-tuple-element.1445), channel_id=1, source_target_pairs={{0,4},{4,8},{8,12},{1,5},{5,9},{9,13},{2,6},{6,10},{10,14},{3,7},{... | collective-permute-start | bytes 393224 | tf_op jit(solution)/shard_map/while/body/eval_jaxpr/ppermute | solution.py:16
  42.1 1.5 collective-permute-done.1
  43.8 18.9 %multiply_subtract_fusion.10 = (f32[2,4,8,512]{3,2,1,0:T(8,128)S(1)}, f32[2,4,8,512]{3,2,1,0:T(8,128)S(1)}, f32[2,4,8,512]{3,2,1,0:T(8,128)S(1)}) fusion(f32[4,8,512]{2,1,0:T(8,128)S(1)} %get-tuple-element.1344, f32[4,8,512]{2,1,0:T(8,128)S(1)} %get-tuple-element.1345, f32[4]{0:T(128)S(1)} %get-tuple-element.1346, f32[4]{0:T(128)S(1)} %get-tuple-element.1347, ...), kind=kLoop, calls=%fused_computation.173.clone.1 | loop fusion | flops 21757952 | bytes 2835456 | tf_op jit(solution)/shard_map/while/body/eval_jaxpr/sub | solution.py:45
  62.8 1.3 collective-permute-start.2
  65.3 1.3 collective-permute-start
  66.6 5.0 %collective-permute-start.1 = (f32[2,4,4,1024]{3,2,1,0:T(4,128)S(1)}, f32[2,4,4,1024]{3,2,1,0:T(4,128)S(1)}, u32[]{:S(2)}, u32[]{:S(2)}) collective-permute-start(f32[2,4,4,1024]{3,2,1,0:T(4,128)S(1)} %get-tuple-element.1445), channel_id=1, source_target_pairs={{0,4},{4,8},{8,12},{1,5},{5,9},{9,13},{2,6},{6,10},{10,14},{3,7},{... | collective-permute-start | bytes 393224 | tf_op jit(solution)/shard_map/while/body/eval_jaxpr/ppermute | solution.py:16
  72.6 1.5 collective-permute-done.1
  74.3 18.9 %multiply_subtract_fusion.10 = (f32[2,4,8,512]{3,2,1,0:T(8,128)S(1)}, f32[2,4,8,512]{3,2,1,0:T(8,128)S(1)}, f32[2,4,8,512]{3,2,1,0:T(8,128)S(1)}) fusion(f32[4,8,512]{2,1,0:T(8,128)S(1)} %get-tuple-element.1344, f32[4,8,512]{2,1,0:T(8,128)S(1)} %get-tuple-element.1345, f32[4]{0:T(128)S(1)} %get-tuple-element.1346, f32[4]{0:T(128)S(1)} %get-tuple-element.1347, ...), kind=kLoop, calls=%fused_computation.173.clone.1 | loop fusion | flops 21757952 | bytes 2835456 | tf_op jit(solution)/shard_map/while/body/eval_jaxpr/sub | solution.py:45
  93.3 5.4 %collective-permute-start.2 = (f32[2,4,8,1024]{3,2,1,0:T(8,128)S(1)}, f32[2,4,8,1024]{3,2,1,0:T(8,128)S(1)}, u32[]{:S(2)}, u32[]{:S(2)}) collective-permute-start(f32[2,4,8,1024]{3,2,1,0:T(8,128)S(1)} %pad_maximum_fusion.17), channel_id=1, source_target_pairs={{0,1},{1,2},{2,3},{4,5},{5,6},{6,7},{8,9},{9,10},{10,11},{12,13},{... | collective-permute-start | bytes 786440 | tf_op jit(solution)/shard_map/while/body/eval_jaxpr/ppermute | solution.py:25
  100.0 1.3 collective-permute-start
  101.3 4.7 %collective-permute-start.1 = (f32[2,4,4,1024]{3,2,1,0:T(4,128)S(1)}, f32[2,4,4,1024]{3,2,1,0:T(4,128)S(1)}, u32[]{:S(2)}, u32[]{:S(2)}) collective-permute-start(f32[2,4,4,1024]{3,2,1,0:T(4,128)S(1)} %get-tuple-element.1445), channel_id=1, source_target_pairs={{0,4},{4,8},{8,12},{1,5},{5,9},{9,13},{2,6},{6,10},{10,14},{3,7},{... | collective-permute-start | bytes 393224 | tf_op jit(solution)/shard_map/while/body/eval_jaxpr/ppermute | solution.py:16
  107.0 1.5 collective-permute-done.1
  108.7 18.9 %multiply_subtract_fusion.10 = (f32[2,4,8,512]{3,2,1,0:T(8,128)S(1)}, f32[2,4,8,512]{3,2,1,0:T(8,128)S(1)}, f32[2,4,8,512]{3,2,1,0:T(8,128)S(1)}) fusion(f32[4,8,512]{2,1,0:T(8,128)S(1)} %get-tuple-element.1344, f32[4,8,512]{2,1,0:T(8,128)S(1)} %get-tuple-element.1345, f32[4]{0:T(128)S(1)} %get-tuple-element.1346, f32[4]{0:T(128)S(1)} %get-tuple-element.1347, ...), kind=kLoop, calls=%fused_computation.173.clone.1 | loop fusion | flops 21757952 | bytes 2835456 | tf_op jit(solution)/shard_map/while/body/eval_jaxpr/sub | solution.py:45
  127.7 6.9 %collective-permute-start.2 = (f32[2,4,8,1024]{3,2,1,0:T(8,128)S(1)}, f32[2,4,8,1024]{3,2,1,0:T(8,128)S(1)}, u32[]{:S(2)}, u32[]{:S(2)}) collective-permute-start(f32[2,4,8,1024]{3,2,1,0:T(8,128)S(1)} %pad_maximum_fusion.17), channel_id=1, source_target_pairs={{0,1},{1,2},{2,3},{4,5},{5,6},{6,7},{8,9},{9,10},{10,11},{12,13},{... | collective-permute-start | bytes 786440 | tf_op jit(solution)/shard_map/while/body/eval_jaxpr/ppermute | solution.py:25
  135.8 4.1 %collective-permute-start.6 = (f32[2,4,4,1024]{3,2,1,0:T(4,128)S(1)}, f32[2,4,4,1024]{3,2,1,0:T(4,128)S(1)}, u32[]{:S(2)}, u32[]{:S(2)}) collective-permute-start(f32[2,4,4,1024]{3,2,1,0:T(4,128)S(1)} %get-tuple-element.828), channel_id=1, source_target_pairs={{0,4},{4,8},{8,12},{1,5},{5,9},{9,13},{2,6},{6,10},{10,14},{3,7},{... | collective-permute-start | bytes 393224 | tf_op jit(solution)/shard_map/ppermute | solution.py:16
  139.8 1.3 collective-permute-start.7
  145.1 1.6 collective-permute-done.7
  146.9 19.0 %multiply_subtract_fusion.3 = (f32[2,4,8,512]{3,2,1,0:T(8,128)S(1)}, f32[2,4,8,512]{3,2,1,0:T(8,128)S(1)}, f32[2,4,8,512]{3,2,1,0:T(8,128)S(1)}) fusion(f32[4,8,512]{2,1,0:T(8,128)S(1)} %get-tuple-element.922, f32[4,8,512]{2,1,0:T(8,128)S(1)} %get-tuple-element.921, f32[4]{0:T(128)S(1)} %get-tuple-element.410, f32[4]{0:T(128)S(1)} %get-tuple-element.409, ...), kind=kLoop, calls=%fused_computation.999 | loop fusion | flops 21757952 | bytes 2835456 | tf_op jit(solution)/shard_map/sub | solution.py:45
  166.0 72.3 %while.29 = (s32[]{:T(128)}, f32[1,4,8,1024]{3,2,1,0:T(8,128)S(1)}, f32[4,1,9,9]{0,3,2,1:T(8,128)S(1)}, f32[1,8,1024]{2,1,0:T(8,128)S(1)}, f32[1,4,8,1024]{3,2,1...) while((s32[]{:T(128)}, f32[1,4,8,1024]{3,2,1,0:T(8,128)S(1)}, ...), condition=%wide.region_4.5_spmd.clone.clone, body=%wide.region_3.4_spmd.clone.clone.sunk | while | flops 11239426 | bytes 7006565 | solution.py:128
  166.4 3.9 %collective-permute-start.3 = (f32[1,4,4,1024]{3,2,1,0:T(4,128)S(1)}, f32[1,4,4,1024]{3,2,1,0:T(4,128)S(1)}, u32[]{:S(2)}, u32[]{:S(2)}) collective-permute-start(f32[1,4,4,1024]{3,2,1,0:T(4,128)S(1)} %get-tuple-element.1525), channel_id=1, source_target_pairs={{0,4},{4,8},{8,12},{1,5},{5,9},{9,13},{2,6},{6,10},{10,14},{3,7},{... | collective-permute-start | bytes 196616 | tf_op jit(solution)/shard_map/while/body/eval_jaxpr/ppermute | solution.py:16
  170.3 1.3 collective-permute-start.4
  172.2 4.3 %collective-permute-done.4 = f32[1,4,4,1024]{3,2,1,0:T(4,128)S(1)} collective-permute-done((f32[1,4,4,1024]{3,2,1,0:T(4,128)S(1)}, f32[1,4,4,1024]{3,2,1,0:T(4,128)S(1)}, u32[]{:S(2)}, u32[]{:S(2)}) %collective-permute-start.4) | collective-permute-done | bytes 65568 | tf_op jit(solution)/shard_map/while/body/eval_jaxpr/ppermute | solution.py:17
  176.6 3.7 %multiply_subtract_fusion.11 = f32[1,4,8,512]{3,2,1,0:T(8,128)S(1)} fusion(f32[1,4,8,512]{3,2,1,0:T(8,128)S(1)} %get-tuple-element.1523, f32[1,4,8,512]{3,2,1,0:T(8,128)S(1)} %get-tuple-element.1524, f32[1,4,12,1024]{3,2,1,0:T(8,128)S(1)} %get-tuple-element.1527, f32[1,4,12,1024]{3,2,1,0:T(8,128)S(1)} %get-tuple-element.1528, ...), kind=kLoop, calls=%fused_computation.510.clone.1 | loop fusion | flops 5292032 | bytes 1509920 | tf_op jit(solution)/shard_map/while/body/eval_jaxpr/sub | solution.py:72
  180.2 3.7 %multiply_add_fusion.21 = f32[1,4,8,512]{3,2,1,0:T(8,128)S(1)} fusion(f32[1,4,8,512]{3,2,1,0:T(8,128)S(1)} %get-tuple-element.1523, f32[1,4,8,512]{3,2,1,0:T(8,128)S(1)} %get-tuple-element.1524, f32[1,4,12,1024]{3,2,1,0:T(8,128)S(1)} %get-tuple-element.1527, f32[1,4,12,1024]{3,2,1,0:T(8,128)S(1)} %get-tuple-element.1528, ...), kind=kLoop, calls=%fused_computation.508.clone.1 | loop fusion | flops 5292032 | bytes 1509920 | tf_op jit(solution)/shard_map/while/body/eval_jaxpr/add | solution.py:73
  183.9 1.3 collective-permute-start.5
  185.2 4.9 %collective-permute-done.5 = f32[1,4,8,1024]{3,2,1,0:T(8,128)S(1)} collective-permute-done((f32[1,4,8,1024]{3,2,1,0:T(8,128)S(1)}, f32[1,4,8,1024]{3,2,1,0:T(8,128)S(1)}, u32[]{:S(2)}, u32[]{:S(2)}) %collective-permute-start.5) | collective-permute-done | bytes 131104 | tf_op jit(solution)/shard_map/while/body/eval_jaxpr/ppermute | solution.py:25
  190.5 3.6 %collective-permute-start.3 = (f32[1,4,4,1024]{3,2,1,0:T(4,128)S(1)}, f32[1,4,4,1024]{3,2,1,0:T(4,128)S(1)}, u32[]{:S(2)}, u32[]{:S(2)}) collective-permute-start(f32[1,4,4,1024]{3,2,1,0:T(4,128)S(1)} %get-tuple-element.1525), channel_id=1, source_target_pairs={{0,4},{4,8},{8,12},{1,5},{5,9},{9,13},{2,6},{6,10},{10,14},{3,7},{... | collective-permute-start | bytes 196616 | tf_op jit(solution)/shard_map/while/body/eval_jaxpr/ppermute | solution.py:16
  194.1 1.3 collective-permute-start.4
  196.0 4.3 %collective-permute-done.4 = f32[1,4,4,1024]{3,2,1,0:T(4,128)S(1)} collective-permute-done((f32[1,4,4,1024]{3,2,1,0:T(4,128)S(1)}, f32[1,4,4,1024]{3,2,1,0:T(4,128)S(1)}, u32[]{:S(2)}, u32[]{:S(2)}) %collective-permute-start.4) | collective-permute-done | bytes 65568 | tf_op jit(solution)/shard_map/while/body/eval_jaxpr/ppermute | solution.py:17
  200.4 3.7 %multiply_subtract_fusion.11 = f32[1,4,8,512]{3,2,1,0:T(8,128)S(1)} fusion(f32[1,4,8,512]{3,2,1,0:T(8,128)S(1)} %get-tuple-element.1523, f32[1,4,8,512]{3,2,1,0:T(8,128)S(1)} %get-tuple-element.1524, f32[1,4,12,1024]{3,2,1,0:T(8,128)S(1)} %get-tuple-element.1527, f32[1,4,12,1024]{3,2,1,0:T(8,128)S(1)} %get-tuple-element.1528, ...), kind=kLoop, calls=%fused_computation.510.clone.1 | loop fusion | flops 5292032 | bytes 1509920 | tf_op jit(solution)/shard_map/while/body/eval_jaxpr/sub | solution.py:72
  204.1 3.7 %multiply_add_fusion.21 = f32[1,4,8,512]{3,2,1,0:T(8,128)S(1)} fusion(f32[1,4,8,512]{3,2,1,0:T(8,128)S(1)} %get-tuple-element.1523, f32[1,4,8,512]{3,2,1,0:T(8,128)S(1)} %get-tuple-element.1524, f32[1,4,12,1024]{3,2,1,0:T(8,128)S(1)} %get-tuple-element.1527, f32[1,4,12,1024]{3,2,1,0:T(8,128)S(1)} %get-tuple-element.1528, ...), kind=kLoop, calls=%fused_computation.508.clone.1 | loop fusion | flops 5292032 | bytes 1509920 | tf_op jit(solution)/shard_map/while/body/eval_jaxpr/add | solution.py:73
  207.8 1.3 collective-permute-start.5
  209.1 6.9 %collective-permute-done.5 = f32[1,4,8,1024]{3,2,1,0:T(8,128)S(1)} collective-permute-done((f32[1,4,8,1024]{3,2,1,0:T(8,128)S(1)}, f32[1,4,8,1024]{3,2,1,0:T(8,128)S(1)}, u32[]{:S(2)}, u32[]{:S(2)}) %collective-permute-start.5) | collective-permute-done | bytes 131104 | tf_op jit(solution)/shard_map/while/body/eval_jaxpr/ppermute | solution.py:25
  216.4 3.3 %collective-permute-start.3 = (f32[1,4,4,1024]{3,2,1,0:T(4,128)S(1)}, f32[1,4,4,1024]{3,2,1,0:T(4,128)S(1)}, u32[]{:S(2)}, u32[]{:S(2)}) collective-permute-start(f32[1,4,4,1024]{3,2,1,0:T(4,128)S(1)} %get-tuple-element.1525), channel_id=1, source_target_pairs={{0,4},{4,8},{8,12},{1,5},{5,9},{9,13},{2,6},{6,10},{10,14},{3,7},{... | collective-permute-start | bytes 196616 | tf_op jit(solution)/shard_map/while/body/eval_jaxpr/ppermute | solution.py:16
  221.6 4.3 %collective-permute-done.4 = f32[1,4,4,1024]{3,2,1,0:T(4,128)S(1)} collective-permute-done((f32[1,4,4,1024]{3,2,1,0:T(4,128)S(1)}, f32[1,4,4,1024]{3,2,1,0:T(4,128)S(1)}, u32[]{:S(2)}, u32[]{:S(2)}) %collective-permute-start.4) | collective-permute-done | bytes 65568 | tf_op jit(solution)/shard_map/while/body/eval_jaxpr/ppermute | solution.py:17
  226.0 3.7 %multiply_subtract_fusion.11 = f32[1,4,8,512]{3,2,1,0:T(8,128)S(1)} fusion(f32[1,4,8,512]{3,2,1,0:T(8,128)S(1)} %get-tuple-element.1523, f32[1,4,8,512]{3,2,1,0:T(8,128)S(1)} %get-tuple-element.1524, f32[1,4,12,1024]{3,2,1,0:T(8,128)S(1)} %get-tuple-element.1527, f32[1,4,12,1024]{3,2,1,0:T(8,128)S(1)} %get-tuple-element.1528, ...), kind=kLoop, calls=%fused_computation.510.clone.1 | loop fusion | flops 5292032 | bytes 1509920 | tf_op jit(solution)/shard_map/while/body/eval_jaxpr/sub | solution.py:72
  229.7 3.7 %multiply_add_fusion.21 = f32[1,4,8,512]{3,2,1,0:T(8,128)S(1)} fusion(f32[1,4,8,512]{3,2,1,0:T(8,128)S(1)} %get-tuple-element.1523, f32[1,4,8,512]{3,2,1,0:T(8,128)S(1)} %get-tuple-element.1524, f32[1,4,12,1024]{3,2,1,0:T(8,128)S(1)} %get-tuple-element.1527, f32[1,4,12,1024]{3,2,1,0:T(8,128)S(1)} %get-tuple-element.1528, ...), kind=kLoop, calls=%fused_computation.508.clone.1 | loop fusion | flops 5292032 | bytes 1509920 | tf_op jit(solution)/shard_map/while/body/eval_jaxpr/add | solution.py:73
  234.7 3.6 %collective-permute-done.5 = f32[1,4,8,1024]{3,2,1,0:T(8,128)S(1)} collective-permute-done((f32[1,4,8,1024]{3,2,1,0:T(8,128)S(1)}, f32[1,4,8,1024]{3,2,1,0:T(8,128)S(1)}, u32[]{:S(2)}, u32[]{:S(2)}) %collective-permute-start.5) | collective-permute-done | bytes 131104 | tf_op jit(solution)/shard_map/while/body/eval_jaxpr/ppermute | solution.py:25
  238.6 2.2 collective-permute-start.8
  240.8 1.5 collective-permute-start.9
  242.9 4.0 %collective-permute-done.9 = f32[1,4,4,1024]{3,2,1,0:T(4,128)S(1)} collective-permute-done((f32[1,4,4,1024]{3,2,1,0:T(4,128)S(1)}, f32[1,4,4,1024]{3,2,1,0:T(4,128)S(1)}, u32[]{:S(2)}, u32[]{:S(2)}) %collective-permute-start.9) | collective-permute-done | bytes 65568 | tf_op jit(solution)/shard_map/ppermute | solution.py:17
  247.1 3.6 %multiply_subtract_fusion.5 = f32[1,4,8,512]{3,2,1,0:T(8,128)S(1)} fusion(f32[1,4,8,512]{3,2,1,0:T(8,128)S(1)} %get-tuple-element.831, f32[1,4,8,512]{3,2,1,0:T(8,128)S(1)} %get-tuple-element.830, f32[1,4,12,1024]{3,2,1,0:T(8,128)S(1)} %get-tuple-element.835, f32[1,4,12,1024]{3,2,1,0:T(8,128)S(1)} %get-tuple-element.834, ...), kind=kLoop, calls=%fused_computation.1022 | loop fusion | flops 5292032 | bytes 1509920 | tf_op jit(solution)/shard_map/sub | solution.py:72
  250.8 3.7 %multiply_add_fusion.13 = f32[1,4,8,512]{3,2,1,0:T(8,128)S(1)} fusion(f32[1,4,8,512]{3,2,1,0:T(8,128)S(1)} %get-tuple-element.831, f32[1,4,8,512]{3,2,1,0:T(8,128)S(1)} %get-tuple-element.830, f32[1,4,12,1024]{3,2,1,0:T(8,128)S(1)} %get-tuple-element.835, f32[1,4,12,1024]{3,2,1,0:T(8,128)S(1)} %get-tuple-element.834, ...), kind=kLoop, calls=%fused_computation.1020 | loop fusion | flops 5292032 | bytes 1509920 | tf_op jit(solution)/shard_map/add | solution.py:73
  254.5 9.1 %all_gather.12 = f32[4,4,8,1024]{3,2,1,0:T(8,128)S(1)} all-gather(f32[1,4,8,1024]{3,2,1,0:T(8,128)S(1)} %maximum_select_fusion.1), channel_id=1, replica_groups=mesh['shots'=2,'lat'=4,'depth'=4] {'depth'}, dimensions={0}, use_global_device_ids=true | all-gather | bytes 655360 | tf_op jit(solution)/shard_map/all_gather | solution.py:30
  (186 shorter events, 23.9 us)
Async XLA Ops:
  0.7 0.7 copy-start.7
  2.5 0.7 copy-start.5
  2.6 0.7 copy-start.6
  32.1 0.9 copy-start.1
  33.1 0.7 copy-start.4
  33.1 1.4 copy-start
  34.5 0.7 copy-start.2
  35.2 6.9 %collective-permute-start = (f32[2,4,4,1024]{3,2,1,0:T(4,128)S(1)}, f32[2,4,4,1024]{3,2,1,0:T(4,128)S(1)}, u32[]{:S(2)}, u32[]{:S(2)}) collective-permute-start(f32[2,4,4,1024]{3,2,1,0:T(4,128)S(1)} %get-tuple-element.1354), channel_id=1, source_target_pairs={{4,0},{8,4},{12,8},{5,1},{9,5},{13,9},{6,2},{10,6},{14,10},{7,3},{... | collective-permute-start | bytes 393224 | tf_op jit(solution)/shard_map/while/body/eval_jaxpr/ppermute | solution.py:17
  36.5 7.1 %collective-permute-start.1 = (f32[2,4,4,1024]{3,2,1,0:T(4,128)S(1)}, f32[2,4,4,1024]{3,2,1,0:T(4,128)S(1)}, u32[]{:S(2)}, u32[]{:S(2)}) collective-permute-start(f32[2,4,4,1024]{3,2,1,0:T(4,128)S(1)} %get-tuple-element.1445), channel_id=1, source_target_pairs={{0,4},{4,8},{8,12},{1,5},{5,9},{9,13},{2,6},{6,10},{10,14},{3,7},{... | collective-permute-start | bytes 393224 | tf_op jit(solution)/shard_map/while/body/eval_jaxpr/ppermute | solution.py:16
  62.8 2.4 collective-permute-start.2
  65.3 7.3 %collective-permute-start = (f32[2,4,4,1024]{3,2,1,0:T(4,128)S(1)}, f32[2,4,4,1024]{3,2,1,0:T(4,128)S(1)}, u32[]{:S(2)}, u32[]{:S(2)}) collective-permute-start(f32[2,4,4,1024]{3,2,1,0:T(4,128)S(1)} %get-tuple-element.1354), channel_id=1, source_target_pairs={{4,0},{8,4},{12,8},{5,1},{9,5},{13,9},{6,2},{10,6},{14,10},{7,3},{... | collective-permute-start | bytes 393224 | tf_op jit(solution)/shard_map/while/body/eval_jaxpr/ppermute | solution.py:17
  66.6 7.5 %collective-permute-start.1 = (f32[2,4,4,1024]{3,2,1,0:T(4,128)S(1)}, f32[2,4,4,1024]{3,2,1,0:T(4,128)S(1)}, u32[]{:S(2)}, u32[]{:S(2)}) collective-permute-start(f32[2,4,4,1024]{3,2,1,0:T(4,128)S(1)} %get-tuple-element.1445), channel_id=1, source_target_pairs={{0,4},{4,8},{8,12},{1,5},{5,9},{9,13},{2,6},{6,10},{10,14},{3,7},{... | collective-permute-start | bytes 393224 | tf_op jit(solution)/shard_map/while/body/eval_jaxpr/ppermute | solution.py:16
  93.3 6.6 %collective-permute-start.2 = (f32[2,4,8,1024]{3,2,1,0:T(8,128)S(1)}, f32[2,4,8,1024]{3,2,1,0:T(8,128)S(1)}, u32[]{:S(2)}, u32[]{:S(2)}) collective-permute-start(f32[2,4,8,1024]{3,2,1,0:T(8,128)S(1)} %pad_maximum_fusion.17), channel_id=1, source_target_pairs={{0,1},{1,2},{2,3},{4,5},{5,6},{6,7},{8,9},{9,10},{10,11},{12,13},{... | collective-permute-start | bytes 786440 | tf_op jit(solution)/shard_map/while/body/eval_jaxpr/ppermute | solution.py:25
  100.0 7.0 %collective-permute-start = (f32[2,4,4,1024]{3,2,1,0:T(4,128)S(1)}, f32[2,4,4,1024]{3,2,1,0:T(4,128)S(1)}, u32[]{:S(2)}, u32[]{:S(2)}) collective-permute-start(f32[2,4,4,1024]{3,2,1,0:T(4,128)S(1)} %get-tuple-element.1354), channel_id=1, source_target_pairs={{4,0},{8,4},{12,8},{5,1},{9,5},{13,9},{6,2},{10,6},{14,10},{7,3},{... | collective-permute-start | bytes 393224 | tf_op jit(solution)/shard_map/while/body/eval_jaxpr/ppermute | solution.py:17
  101.3 7.2 %collective-permute-start.1 = (f32[2,4,4,1024]{3,2,1,0:T(4,128)S(1)}, f32[2,4,4,1024]{3,2,1,0:T(4,128)S(1)}, u32[]{:S(2)}, u32[]{:S(2)}) collective-permute-start(f32[2,4,4,1024]{3,2,1,0:T(4,128)S(1)} %get-tuple-element.1445), channel_id=1, source_target_pairs={{0,4},{4,8},{8,12},{1,5},{5,9},{9,13},{2,6},{6,10},{10,14},{3,7},{... | collective-permute-start | bytes 393224 | tf_op jit(solution)/shard_map/while/body/eval_jaxpr/ppermute | solution.py:16
  127.7 8.0 %collective-permute-start.2 = (f32[2,4,8,1024]{3,2,1,0:T(8,128)S(1)}, f32[2,4,8,1024]{3,2,1,0:T(8,128)S(1)}, u32[]{:S(2)}, u32[]{:S(2)}) collective-permute-start(f32[2,4,8,1024]{3,2,1,0:T(8,128)S(1)} %pad_maximum_fusion.17), channel_id=1, source_target_pairs={{0,1},{1,2},{2,3},{4,5},{5,6},{6,7},{8,9},{9,10},{10,11},{12,13},{... | collective-permute-start | bytes 786440 | tf_op jit(solution)/shard_map/while/body/eval_jaxpr/ppermute | solution.py:25
  135.8 9.4 %collective-permute-start.6 = (f32[2,4,4,1024]{3,2,1,0:T(4,128)S(1)}, f32[2,4,4,1024]{3,2,1,0:T(4,128)S(1)}, u32[]{:S(2)}, u32[]{:S(2)}) collective-permute-start(f32[2,4,4,1024]{3,2,1,0:T(4,128)S(1)} %get-tuple-element.828), channel_id=1, source_target_pairs={{0,4},{4,8},{8,12},{1,5},{5,9},{9,13},{2,6},{6,10},{10,14},{3,7},{... | collective-permute-start | bytes 393224 | tf_op jit(solution)/shard_map/ppermute | solution.py:16
  139.8 6.9 %collective-permute-start.7 = (f32[2,4,4,1024]{3,2,1,0:T(4,128)S(1)}, f32[2,4,4,1024]{3,2,1,0:T(4,128)S(1)}, u32[]{:S(2)}, u32[]{:S(2)}) collective-permute-start(f32[2,4,4,1024]{3,2,1,0:T(4,128)S(1)} %get-tuple-element.829), channel_id=1, source_target_pairs={{4,0},{8,4},{12,8},{5,1},{9,5},{13,9},{6,2},{10,6},{14,10},{7,3},{... | collective-permute-start | bytes 393224 | tf_op jit(solution)/shard_map/ppermute | solution.py:17
  144.1 0.7 copy-start.3
  166.4 5.8 %collective-permute-start.3 = (f32[1,4,4,1024]{3,2,1,0:T(4,128)S(1)}, f32[1,4,4,1024]{3,2,1,0:T(4,128)S(1)}, u32[]{:S(2)}, u32[]{:S(2)}) collective-permute-start(f32[1,4,4,1024]{3,2,1,0:T(4,128)S(1)} %get-tuple-element.1525), channel_id=1, source_target_pairs={{0,4},{4,8},{8,12},{1,5},{5,9},{9,13},{2,6},{6,10},{10,14},{3,7},{... | collective-permute-start | bytes 196616 | tf_op jit(solution)/shard_map/while/body/eval_jaxpr/ppermute | solution.py:16
  170.3 6.2 %collective-permute-start.4 = (f32[1,4,4,1024]{3,2,1,0:T(4,128)S(1)}, f32[1,4,4,1024]{3,2,1,0:T(4,128)S(1)}, u32[]{:S(2)}, u32[]{:S(2)}) collective-permute-start(f32[1,4,4,1024]{3,2,1,0:T(4,128)S(1)} %get-tuple-element.1526), channel_id=1, source_target_pairs={{4,0},{8,4},{12,8},{5,1},{9,5},{13,9},{6,2},{10,6},{14,10},{7,3},{... | collective-permute-start | bytes 196616 | tf_op jit(solution)/shard_map/while/body/eval_jaxpr/ppermute | solution.py:17
  183.9 6.2 %collective-permute-start.5 = (f32[1,4,8,1024]{3,2,1,0:T(8,128)S(1)}, f32[1,4,8,1024]{3,2,1,0:T(8,128)S(1)}, u32[]{:S(2)}, u32[]{:S(2)}) collective-permute-start(f32[1,4,8,1024]{3,2,1,0:T(8,128)S(1)} %pad_maximum_fusion.19), channel_id=1, source_target_pairs={{1,0},{2,1},{3,2},{5,4},{6,5},{7,6},{9,8},{10,9},{11,10},{13,12},{... | collective-permute-start | bytes 393224 | tf_op jit(solution)/shard_map/while/body/eval_jaxpr/ppermute | solution.py:25
  190.5 5.5 %collective-permute-start.3 = (f32[1,4,4,1024]{3,2,1,0:T(4,128)S(1)}, f32[1,4,4,1024]{3,2,1,0:T(4,128)S(1)}, u32[]{:S(2)}, u32[]{:S(2)}) collective-permute-start(f32[1,4,4,1024]{3,2,1,0:T(4,128)S(1)} %get-tuple-element.1525), channel_id=1, source_target_pairs={{0,4},{4,8},{8,12},{1,5},{5,9},{9,13},{2,6},{6,10},{10,14},{3,7},{... | collective-permute-start | bytes 196616 | tf_op jit(solution)/shard_map/while/body/eval_jaxpr/ppermute | solution.py:16
  194.1 6.2 %collective-permute-start.4 = (f32[1,4,4,1024]{3,2,1,0:T(4,128)S(1)}, f32[1,4,4,1024]{3,2,1,0:T(4,128)S(1)}, u32[]{:S(2)}, u32[]{:S(2)}) collective-permute-start(f32[1,4,4,1024]{3,2,1,0:T(4,128)S(1)} %get-tuple-element.1526), channel_id=1, source_target_pairs={{4,0},{8,4},{12,8},{5,1},{9,5},{13,9},{6,2},{10,6},{14,10},{7,3},{... | collective-permute-start | bytes 196616 | tf_op jit(solution)/shard_map/while/body/eval_jaxpr/ppermute | solution.py:17
  207.8 8.2 %collective-permute-start.5 = (f32[1,4,8,1024]{3,2,1,0:T(8,128)S(1)}, f32[1,4,8,1024]{3,2,1,0:T(8,128)S(1)}, u32[]{:S(2)}, u32[]{:S(2)}) collective-permute-start(f32[1,4,8,1024]{3,2,1,0:T(8,128)S(1)} %pad_maximum_fusion.19), channel_id=1, source_target_pairs={{1,0},{2,1},{3,2},{5,4},{6,5},{7,6},{9,8},{10,9},{11,10},{13,12},{... | collective-permute-start | bytes 393224 | tf_op jit(solution)/shard_map/while/body/eval_jaxpr/ppermute | solution.py:25
  216.4 5.2 %collective-permute-start.3 = (f32[1,4,4,1024]{3,2,1,0:T(4,128)S(1)}, f32[1,4,4,1024]{3,2,1,0:T(4,128)S(1)}, u32[]{:S(2)}, u32[]{:S(2)}) collective-permute-start(f32[1,4,4,1024]{3,2,1,0:T(4,128)S(1)} %get-tuple-element.1525), channel_id=1, source_target_pairs={{0,4},{4,8},{8,12},{1,5},{5,9},{9,13},{2,6},{6,10},{10,14},{3,7},{... | collective-permute-start | bytes 196616 | tf_op jit(solution)/shard_map/while/body/eval_jaxpr/ppermute | solution.py:16
  219.7 6.2 %collective-permute-start.4 = (f32[1,4,4,1024]{3,2,1,0:T(4,128)S(1)}, f32[1,4,4,1024]{3,2,1,0:T(4,128)S(1)}, u32[]{:S(2)}, u32[]{:S(2)}) collective-permute-start(f32[1,4,4,1024]{3,2,1,0:T(4,128)S(1)} %get-tuple-element.1526), channel_id=1, source_target_pairs={{4,0},{8,4},{12,8},{5,1},{9,5},{13,9},{6,2},{10,6},{14,10},{7,3},{... | collective-permute-start | bytes 196616 | tf_op jit(solution)/shard_map/while/body/eval_jaxpr/ppermute | solution.py:17
  233.4 4.9 %collective-permute-start.5 = (f32[1,4,8,1024]{3,2,1,0:T(8,128)S(1)}, f32[1,4,8,1024]{3,2,1,0:T(8,128)S(1)}, u32[]{:S(2)}, u32[]{:S(2)}) collective-permute-start(f32[1,4,8,1024]{3,2,1,0:T(8,128)S(1)} %pad_maximum_fusion.19), channel_id=1, source_target_pairs={{1,0},{2,1},{3,2},{5,4},{6,5},{7,6},{9,8},{10,9},{11,10},{13,12},{... | collective-permute-start | bytes 393224 | tf_op jit(solution)/shard_map/while/body/eval_jaxpr/ppermute | solution.py:25
  238.6 4.3 %collective-permute-start.8 = (f32[1,4,4,1024]{3,2,1,0:T(4,128)S(1)}, f32[1,4,4,1024]{3,2,1,0:T(4,128)S(1)}, u32[]{:S(2)}, u32[]{:S(2)}) collective-permute-start(f32[1,4,4,1024]{3,2,1,0:T(4,128)S(1)} %get-tuple-element.836), channel_id=1, source_target_pairs={{0,4},{4,8},{8,12},{1,5},{5,9},{9,13},{2,6},{6,10},{10,14},{3,7},{... | collective-permute-start | bytes 196616 | tf_op jit(solution)/shard_map/ppermute | solution.py:16
  240.8 6.2 %collective-permute-start.9 = (f32[1,4,4,1024]{3,2,1,0:T(4,128)S(1)}, f32[1,4,4,1024]{3,2,1,0:T(4,128)S(1)}, u32[]{:S(2)}, u32[]{:S(2)}) collective-permute-start(f32[1,4,4,1024]{3,2,1,0:T(4,128)S(1)} %get-tuple-element.837), channel_id=1, source_target_pairs={{4,0},{8,4},{12,8},{5,1},{9,5},{13,9},{6,2},{10,6},{14,10},{7,3},{... | collective-permute-start | bytes 196616 | tf_op jit(solution)/shard_map/ppermute | solution.py:17
